TPU v7x, 32 devices: a whole 2x2x4 slice. The times are simulated.
32 devices in a mesh: ens: 2 (over y), lon: 4 (over z), lat: 2 (over x), lev: 2 (over core).
Axes of the slice: x: 2, y: 2, z: 4, core: 2. Of those that a mesh axis runs over, the one named last changes fastest.
Arguments:
- state: float32 [4, 24, 32, 256], P('ens', 'lev', 'lon', 'lat'), parts along dimension 0, may hold values from -6 to 6
- land_sea: int32 [24, 32, 256], P('lev', 'lon', 'lat'), may hold values 0 or 1
- east_speed: float32 [48, 32, 256], P(('ens', 'lev'), 'lon', 'lat'), parts along dimension 0, may hold values from -0.12 to 0.12
- north_speed: float32 [48, 32, 256], P(('ens', 'lev'), 'lon', 'lat'), parts along dimension 0, may hold values from -0.12 to 0.12
- w_in: float32 [6, 256], replicated, may hold values from -2.5 to 2.5
- b_in: float32 [256], replicated, may hold values from -3 to 3
- w_out: float32 [256, 2], replicated, may hold values from -0.375 to 0.375
- b_out: float32 [2], replicated, may hold values from -3 to 3
- cotangent: float32 [4, 24, 32, 256], P('ens', 'lev', 'lon', 'lat'), parts along dimension 0, may hold values from -6 to 6
Outputs:
- grad_state: float32 [4, 24, 32, 256], P('ens', 'lev', 'lon', 'lat'), parts along dimension 0
- grad_w_in: float32 [12, 256], P('ens'), parts along dimension 0
- grad_b_in: float32 [512], P('ens'), parts along dimension 0
- grad_w_out: float32 [512, 2], P('ens'), parts along dimension 0
- grad_b_out: float32 [4], P('ens'), parts along dimension 0
There are 2 independent parts, one for each index of `ens`. A program takes and returns all parts, laid end to end along the dimension named above; an argument that names none is the same for every part. Nothing has to cross between parts.
All inputs are finite; a program needn't handle non-finite values. No bound on the sum of `land_sea` on one device may be relied on, other than what follows from the above.
Results may differ from a plain program's by a relative error of at most 0.00027.
Values sent between devices are 32-bit elements; how exact they have to be, the bound alone decides.
A program may use at most 64 MiB of HBM per device.

v0:
```python
import jax
import jax.numpy as jnp
from jax import lax
from jax.sharding import PartitionSpec as P

HIGH = lax.Precision.HIGHEST


def padded_2(cells, sides, width):
    for axis, dim in sides:
        count = lax.axis_size(axis)
        head = lax.slice_in_dim(cells, 0, width, axis=dim)
        tail = lax.slice_in_dim(cells, cells.shape[dim] - width, cells.shape[dim], axis=dim)
        cells = jnp.concatenate(
            [
                lax.ppermute(tail, axis, [(i, (i + 1) % count) for i in range(count)]),
                cells,
                lax.ppermute(head, axis, [((i + 1) % count, i) for i in range(count)]),
            ],
            axis=dim,
        )
    return cells


def mix_rates(feat, w_in, b_in, w_out, b_out):
    levels = feat.shape[1]
    flat = jnp.moveaxis(feat, 1, 0).reshape(levels, 6, -1)

    @jax.checkpoint
    def one_level(block):
        hidden = jnp.tanh(jnp.dot(w_in.T, block, precision=HIGH) + b_in[:, None])
        out = jnp.dot(w_out.T, hidden, precision=HIGH) + b_out[:, None]
        return jax.nn.sigmoid(out)

    rates = lax.map(one_level, flat)
    rates = jnp.moveaxis(rates, 1, 0).reshape(2, levels, feat.shape[2], feat.shape[3])
    return (0.08 * rates[0], 0.16 * rates[1])


def tracer_step(state_pad, aux_pad, params):

    def part(array, dz, dx, dy):
        nz = array.shape[1] - 2
        nx = array.shape[2] - 2
        ny = array.shape[3] - 2
        return array[:, 1 + dz : 1 + dz + nz, 1 + dx : 1 + dx + nx, 1 + dy : 1 + dy + ny]

    center = part(state_pad, 0, 0, 0)
    mask = aux_pad[0:1]
    ocean = part(mask, 0, 0, 0)[0]
    east = part(aux_pad[1:2], 0, 0, 0)[0]
    north = part(aux_pad[2:3], 0, 0, 0)[0]

    def flux(dz, dx, dy):
        return part(mask, dz, dx, dy) * (part(state_pad, dz, dx, dy) - center)

    vertical = flux(1, 0, 0) + flux(-1, 0, 0)
    xplus = flux(0, 1, 0)
    xminus = flux(0, -1, 0)
    yplus = flux(0, 0, 1)
    yminus = flux(0, 0, -1)
    horizontal = xplus + xminus + yplus + yminus
    advect = (
        jnp.maximum(east, 0.0) * xminus
        - jnp.minimum(east, 0.0) * xplus
        + jnp.maximum(north, 0.0) * yminus
        - jnp.minimum(north, 0.0) * yplus
    )
    feat = jnp.concatenate([center, vertical, horizontal], 0)
    k_h, k_v = mix_rates(feat, params[0], params[1], params[2], params[3])
    return center + ocean * (k_h * horizontal + k_v * vertical + advect)


def close_ends(aux_pad, width):
    inner_z = aux_pad.shape[1] - 2 * width
    inner_y = aux_pad.shape[3] - 2 * width
    level_pos = jnp.arange(inner_z + 2 * width)
    lat_pos = jnp.arange(inner_y + 2 * width)
    low_z = lax.axis_index("lev") == 0
    high_z = lax.axis_index("lev") == lax.axis_size("lev") - 1
    low_y = lax.axis_index("lat") == 0
    high_y = lax.axis_index("lat") == lax.axis_size("lat") - 1
    keep_z = jnp.where(
        (level_pos < width) & low_z | (level_pos >= inner_z + width) & high_z, 0.0, 1.0
    )
    keep_y = jnp.where((lat_pos < width) & low_y | (lat_pos >= inner_y + width) & high_y, 0.0, 1.0)
    mask = aux_pad[0] * keep_z[:, None, None] * keep_y[None, None, :]
    return jnp.concatenate([mask[None], aux_pad[1:]], 0)


def fold_back(grad_pad):
    ext = padded_2(grad_pad, (("lon", 2), ("lat", 3), ("lev", 1)), 1)
    inner = ext[:, 2:-2, 2:-2, 2:-2]
    inner = inner.at[:, :, 0, :].add(ext[:, 2:-2, 0, 2:-2])
    inner = inner.at[:, :, -1, :].add(ext[:, 2:-2, -1, 2:-2])
    inner = inner.at[:, :, :, 0].add(ext[:, 2:-2, 2:-2, 0])
    inner = inner.at[:, :, :, -1].add(ext[:, 2:-2, 2:-2, -1])
    inner = inner.at[:, 0, :, :].add(ext[:, 0, 2:-2, 2:-2])
    inner = inner.at[:, -1, :, :].add(ext[:, -1, 2:-2, 2:-2])
    return inner


def total_grads(terms):
    return lax.psum((terms[0], terms[1], terms[2], terms[3]), ("lon", "lat", "lev"))


def per_device(state, land_sea, east_speed, north_speed, w_in, b_in, w_out, b_out, cotangent):
    ocean_mask = land_sea.astype(jnp.float32)
    speeds = jnp.stack([east_speed, north_speed])

    def stepper(aux_pad):

        def advance(start_pad, wi, bi, wo, bo):
            return tracer_step(start_pad, aux_pad, (wi, bi, wo, bo))

        return advance

    joined = jnp.concatenate([state, ocean_mask[None]], 0)
    padded = padded_2(joined, (("lon", 2), ("lat", 3), ("lev", 1)), 1)
    first_pad = padded[:2]
    speed_pad = jnp.pad(speeds, ((0, 0), (1, 1), (1, 1), (1, 1)))
    aux_pad = close_ends(jnp.concatenate([padded[2:3], speed_pad], 0), 1)
    after_one, back_first = jax.vjp(stepper(aux_pad), first_pad, w_in, b_in, w_out, b_out)
    second_pad = padded_2(after_one, (("lon", 2), ("lat", 3), ("lev", 1)), 1)
    after_two, back_second = jax.vjp(stepper(aux_pad), second_pad, w_in, b_in, w_out, b_out)
    grads_second = back_second(cotangent)
    middle_grad = fold_back(grads_second[0])
    grads_first = back_first(middle_grad)
    start_grad = fold_back(grads_first[0])
    summed_second = total_grads(grads_second[1:])
    summed_first = total_grads(grads_first[1:])
    summed = [summed_second[i] + summed_first[i] for i in range(4)]
    cells = (
        state.shape[1]
        * state.shape[2]
        * state.shape[3]
        * lax.axis_size("lon")
        * lax.axis_size("lat")
        * lax.axis_size("lev")
    )
    factor = float(cells) ** (-0.5)
    return (
        start_grad,
        summed[0] * factor,
        summed[1] * factor,
        summed[2] * factor,
        summed[3] * factor,
    )


def solution(mesh):
    placed = (
        P("ens", "lev", "lon", "lat"),
        P("lev", "lon", "lat"),
        P(("ens", "lev"), "lon", "lat"),
        P(("ens", "lev"), "lon", "lat"),
        P(),
        P(),
        P(),
        P(),
        P("ens", "lev", "lon", "lat"),
    )
    return jax.shard_map(
        per_device,
        mesh=mesh,
        in_specs=placed,
        out_specs=(
            P("ens", "lev", "lon", "lat"),
            P("ens", None),
            P("ens"),
            P("ens", None),
            P("ens"),
        ),
        check_vma=False,
    )
```

profile of v0, /device:TPU:0, one launch (start us, length us, event | category | flops | bytes accessed | tf_op | source)
XLA Modules:
  0.0 335.7 jit_solution(3967119030836334756)
XLA Ops:
  1.6 3.1 collective-permute-start
  4.7 2.1 collective-permute-start.1
  6.8 1.7 collective-permute-done
  10.9 7.9 %collective-permute-done.2 = f32[3,12,10,1]{3,2,1,0:T(8,128)S(1)} collective-permute-done((f32[3,12,10,1]{3,2,1,0:T(8,128)S(1)}, f32[3,12,10,1]{3,2,1,0:T(8,128)S(1)}, u32[]{:S(2)}, u32[]{:S(2)}) %collective-permute-start.2) | collective-permute-done | bytes 1472 | tf_op jit(solution)/shard_map/ppermute | solution.py:16
  18.8 4.1 %collective-permute-done.3 = f32[3,12,10,1]{3,2,1,0:T(8,128)S(1)} collective-permute-done((f32[3,12,10,1]{3,2,1,0:T(8,128)S(1)}, f32[3,12,10,1]{3,2,1,0:T(8,128)S(1)}, u32[]{:S(2)}, u32[]{:S(2)}) %collective-permute-start.3) | collective-permute-done | bytes 1472 | tf_op jit(solution)/shard_map/ppermute | solution.py:18
  26.2 25.0 %while.78 = (s32[]{:T(128)}, f32[12,2,1024]{2,1,0:T(2,128)S(1)}, f32[12,6,1024]{2,1,0:T(8,128)S(1)}, f32[256,6]{0,1:T(8,128)S(1)}, f32[256,1]{0,1:T(1,128)S(1)},...) while((s32[]{:T(128)}, f32[12,2,1024]{2,1,0:T(2,128)S(1)}, f32[12,6,1024]{2,1,0:T(8,128)S(1)}, ...), condition=%wide.region_1.2_spmd, body=%wide.region_0.1_spmd.sunk | while | flops 25436160 | bytes 2149989 | solution.py:35
  52.9 2.7 collective-permute-start.7
  55.6 1.6 collective-permute-done.6
  59.5 5.8 %collective-permute-done.8 = f32[2,12,10,1]{3,2,1,0:T(8,128)S(1)} collective-permute-done((f32[2,12,10,1]{3,2,1,0:T(8,128)S(1)}, f32[2,12,10,1]{3,2,1,0:T(8,128)S(1)}, u32[]{:S(2)}, u32[]{:S(2)}) %collective-permute-start.8) | collective-permute-done | bytes 992 | tf_op jit(solution)/shard_map/ppermute | solution.py:16
  65.3 2.5 collective-permute-done.9
  70.0 25.0 %while.79 = (s32[]{:T(128)}, f32[12,2,1024]{2,1,0:T(2,128)S(1)}, f32[12,6,1024]{2,1,0:T(8,128)S(1)}, f32[256,6]{0,1:T(8,128)S(1)}, f32[256,1]{0,1:T(1,128)S(1)},...) while((s32[]{:T(128)}, f32[12,2,1024]{2,1,0:T(2,128)S(1)}, f32[12,6,1024]{2,1,0:T(8,128)S(1)}, ...), condition=%wide.region_3.4_spmd, body=%wide.region_2.3_spmd.sunk | while | flops 25436160 | bytes 2149989 | solution.py:35
  95.2 66.6 %while.80 = (s32[]{:T(128)}, f32[6,256]{1,0:T(8,128)S(1)}, f32[256]{0:T(256)S(1)}, f32[256,2]{0,1:T(2,128)S(1)}, f32[2]{0:T(128)S(1)}, /*index=5*/f32[12,6,1024]...) while((s32[]{:T(128)}, f32[6,256]{1,0:T(8,128)S(1)}, ...), condition=%wide.region_9.10_spmd.clone, body=%wide.region_6.9_spmd.clone.sunk | while | flops 77091072 | bytes 7560418 | solution.py:35
  162.7 3.8 %collective-permute-start.13 = (f32[2,14,1,130]{3,2,1,0:T(1,128)S(1)}, f32[2,14,1,130]{3,2,1,0:T(1,128)S(1)}, u32[]{:S(2)}, u32[]{:S(2)}) collective-permute-start(f32[2,14,1,130]{3,2,1,0:T(1,128)S(1)} %get-tuple-element.977), channel_id=1, source_target_pairs={{4,0},{8,4},{12,8},{0,12},{5,1},{9,5},{13,9},{1,13},{6,2},{10,6},{... | collective-permute-start | bytes 43688 | tf_op jit(solution)/shard_map/ppermute | solution.py:18
  168.1 4.1 %collective-permute-done.12 = f32[2,14,1,130]{3,2,1,0:T(1,128)S(1)} collective-permute-done((f32[2,14,1,130]{3,2,1,0:T(1,128)S(1)}, f32[2,14,1,130]{3,2,1,0:T(1,128)S(1)}, u32[]{:S(2)}, u32[]{:S(2)}) %collective-permute-start.12) | collective-permute-done | bytes 14592 | tf_op jit(solution)/shard_map/ppermute | solution.py:16
  175.5 8.9 %collective-permute-done.14 = f32[2,14,12,1]{3,2,1,0:T(8,128)S(1)} collective-permute-done((f32[2,14,12,1]{3,2,1,0:T(8,128)}, f32[2,14,12,1]{3,2,1,0:T(8,128)S(1)}, u32[]{:S(2)}, u32[]{:S(2)}) %collective-permute-start.14) | collective-permute-done | bytes 1376 | tf_op jit(solution)/shard_map/ppermute | solution.py:16
  185.5 2.0 scatter-add.45
  188.1 66.6 %while.81 = (s32[]{:T(128)}, f32[6,256]{1,0:T(8,128)S(1)}, f32[256]{0:T(256)S(1)}, f32[256,2]{0,1:T(2,128)S(1)}, f32[2]{0:T(128)S(1)}, /*index=5*/f32[12,6,1024]...) while((s32[]{:T(128)}, f32[6,256]{1,0:T(8,128)S(1)}, ...), condition=%wide.region_15.16_spmd.clone, body=%wide.region_12.15_spmd.clone.sunk | while | flops 77091072 | bytes 7560418 | solution.py:35
  255.0 58.4 %all-reduce.18 = (f32[6,256]{1,0:T(8,128)S(1)}, f32[256]{0:T(256)S(1)}, f32[256,2]{0,1:T(2,128)S(1)}, f32[2]{0:T(128)S(1)}) all-reduce(f32[6,256]{1,0:T(8,128)S(1)} %add.418, f32[256]{0:T(256)S(1)} %add.419, f32[256,2]{0,1:T(2,128)S(1)} %add.420, f32[2]{0:T(128)S(1)} %add.421), channel_id=1, replica_groups=mesh['ens'=2,'lon'=4,'lat'=2,'lev'=2] {'lon','lat','lev'}, use_global_device_ids=true, to_apply=%region_16.17 | all-reduce | flops 2306 | bytes 18448 | tf_op jit(solution)/shard_map/psum | solution.py:104
  315.8 2.0 collective-permute-start.18
  319.7 1.9 collective-permute-done.18
  322.3 2.1 collective-permute-start.21
  324.3 4.7 %collective-permute-done.20 = f32[2,14,12,1]{3,2,1,0:T(8,128)S(1)} collective-permute-done((f32[2,14,12,1]{3,2,1,0:T(8,128)S(1)}, f32[2,14,12,1]{3,2,1,0:T(8,128)S(1)}, u32[]{:S(2)}, u32[]{:S(2)}) %collective-permute-start.20) | collective-permute-done | bytes 1376 | tf_op jit(solution)/shard_map/ppermute | solution.py:16
  329.2 2.2 collective-permute-done.21
  331.8 1.8 scatter-add.55
  (429 shorter events, 209.9 us)
Async XLA Ops:
  1.6 6.9 %collective-permute-start = (f32[3,12,1,128]{3,2,1,0:T(1,128)S(1)}, f32[3,12,1,128]{3,2,1,0:T(1,128)S(1)}, u32[]{:S(2)}, u32[]{:S(2)}) collective-permute-start(f32[3,12,1,128]{3,2,1,0:T(1,128)S(1)} %get-tuple-element.990), channel_id=1, source_target_pairs={{0,4},{4,8},{8,12},{12,0},{1,5},{5,9},{9,13},{13,1},{2,6},{6,10},{... | collective-permute-start | bytes 55304 | tf_op jit(solution)/shard_map/ppermute | solution.py:16
  4.7 4.0 %collective-permute-start.1 = (f32[3,12,1,128]{3,2,1,0:T(1,128)S(1)}, f32[3,12,1,128]{3,2,1,0:T(1,128)S(1)}, u32[]{:S(2)}, u32[]{:S(2)}) collective-permute-start(f32[3,12,1,128]{3,2,1,0:T(1,128)S(1)} %get-tuple-element.991), channel_id=1, source_target_pairs={{4,0},{8,4},{12,8},{0,12},{5,1},{9,5},{13,9},{1,13},{6,2},{10,6},{... | collective-permute-start | bytes 55304 | tf_op jit(solution)/shard_map/ppermute | solution.py:18
  8.8 10.0 %collective-permute-start.2 = (f32[3,12,10,1]{3,2,1,0:T(8,128)S(1)}, f32[3,12,10,1]{3,2,1,0:T(8,128)S(1)}, u32[]{:S(2)}, u32[]{:S(2)}) collective-permute-start(f32[3,12,10,1]{3,2,1,0:T(8,128)S(1)} %get-tuple-element.979), channel_id=1, source_target_pairs={{0,2},{2,0},{1,3},{3,1},{4,6},{6,4},{5,7},{7,5},{8,10},{10,8},{9,1... | collective-permute-start | bytes 4328 | tf_op jit(solution)/shard_map/ppermute | solution.py:16
  10.4 12.5 %collective-permute-start.3 = (f32[3,12,10,1]{3,2,1,0:T(8,128)S(1)}, f32[3,12,10,1]{3,2,1,0:T(8,128)S(1)}, u32[]{:S(2)}, u32[]{:S(2)}) collective-permute-start(f32[3,12,10,1]{3,2,1,0:T(8,128)S(1)} %get-tuple-element.980), channel_id=1, source_target_pairs={{2,0},{0,2},{3,1},{1,3},{6,4},{4,6},{7,5},{5,7},{10,8},{8,10},{11,... | collective-permute-start | bytes 4328 | tf_op jit(solution)/shard_map/ppermute | solution.py:18
  23.0 1.3 collective-permute-start.4
  23.1 1.4 collective-permute-start.5
  51.7 5.5 %collective-permute-start.6 = (f32[2,12,1,128]{3,2,1,0:T(1,128)S(1)}, f32[2,12,1,128]{3,2,1,0:T(1,128)S(1)}, u32[]{:S(2)}, u32[]{:S(2)}) collective-permute-start(f32[2,12,1,128]{3,2,1,0:T(1,128)S(1)} %get-tuple-element.994), channel_id=1, source_target_pairs={{0,4},{4,8},{8,12},{12,0},{1,5},{5,9},{9,13},{13,1},{2,6},{6,10},{... | collective-permute-start | bytes 36872 | tf_op jit(solution)/shard_map/ppermute | solution.py:16
  52.9 4.4 %collective-permute-start.7 = (f32[2,12,1,128]{3,2,1,0:T(1,128)S(1)}, f32[2,12,1,128]{3,2,1,0:T(1,128)S(1)}, u32[]{:S(2)}, u32[]{:S(2)}) collective-permute-start(f32[2,12,1,128]{3,2,1,0:T(1,128)S(1)} %get-tuple-element.995), channel_id=1, source_target_pairs={{4,0},{8,4},{12,8},{0,12},{5,1},{9,5},{13,9},{1,13},{6,2},{10,6},{... | collective-permute-start | bytes 36872 | tf_op jit(solution)/shard_map/ppermute | solution.py:18
  57.4 7.9 %collective-permute-start.8 = (f32[2,12,10,1]{3,2,1,0:T(8,128)S(1)}, f32[2,12,10,1]{3,2,1,0:T(8,128)S(1)}, u32[]{:S(2)}, u32[]{:S(2)}) collective-permute-start(f32[2,12,10,1]{3,2,1,0:T(8,128)S(1)} %get-tuple-element.988), channel_id=1, source_target_pairs={{0,2},{2,0},{1,3},{3,1},{4,6},{6,4},{5,7},{7,5},{8,10},{10,8},{9,1... | collective-permute-start | bytes 2888 | tf_op jit(solution)/shard_map/ppermute | solution.py:16
  58.9 8.8 %collective-permute-start.9 = (f32[2,12,10,1]{3,2,1,0:T(8,128)S(1)}, f32[2,12,10,1]{3,2,1,0:T(8,128)S(1)}, u32[]{:S(2)}, u32[]{:S(2)}) collective-permute-start(f32[2,12,10,1]{3,2,1,0:T(8,128)S(1)} %get-tuple-element.989), channel_id=1, source_target_pairs={{2,0},{0,2},{3,1},{1,3},{6,4},{4,6},{7,5},{5,7},{10,8},{8,10},{11,... | collective-permute-start | bytes 2888 | tf_op jit(solution)/shard_map/ppermute | solution.py:18
  67.9 1.3 collective-permute-start.10
  67.9 1.4 collective-permute-start.11
  162.7 5.4 %collective-permute-start.13 = (f32[2,14,1,130]{3,2,1,0:T(1,128)S(1)}, f32[2,14,1,130]{3,2,1,0:T(1,128)S(1)}, u32[]{:S(2)}, u32[]{:S(2)}) collective-permute-start(f32[2,14,1,130]{3,2,1,0:T(1,128)S(1)} %get-tuple-element.977), channel_id=1, source_target_pairs={{4,0},{8,4},{12,8},{0,12},{5,1},{9,5},{13,9},{1,13},{6,2},{10,6},{... | collective-permute-start | bytes 43688 | tf_op jit(solution)/shard_map/ppermute | solution.py:18
  166.5 5.7 %collective-permute-start.12 = (f32[2,14,1,130]{3,2,1,0:T(1,128)S(1)}, f32[2,14,1,130]{3,2,1,0:T(1,128)S(1)}, u32[]{:S(2)}, u32[]{:S(2)}) collective-permute-start(f32[2,14,1,130]{3,2,1,0:T(1,128)S(1)} %get-tuple-element.978), channel_id=1, source_target_pairs={{0,4},{4,8},{8,12},{12,0},{1,5},{5,9},{9,13},{13,1},{2,6},{6,10},{... | collective-permute-start | bytes 43688 | tf_op jit(solution)/shard_map/ppermute | solution.py:16
  173.1 11.6 %collective-permute-start.15 = (f32[2,14,12,1]{3,2,1,0:T(8,128)S(1)}, f32[2,14,12,1]{3,2,1,0:T(8,128)S(1)}, u32[]{:S(2)}, u32[]{:S(2)}) collective-permute-start(f32[2,14,12,1]{3,2,1,0:T(8,128)S(1)} %get-tuple-element.975), channel_id=1, source_target_pairs={{2,0},{0,2},{3,1},{1,3},{6,4},{4,6},{7,5},{5,7},{10,8},{8,10},{11,... | collective-permute-start | bytes 4040 | tf_op jit(solution)/shard_map/ppermute | solution.py:18
  174.6 9.8 %collective-permute-start.14 = (f32[2,14,12,1]{3,2,1,0:T(8,128)}, f32[2,14,12,1]{3,2,1,0:T(8,128)S(1)}, u32[]{:S(2)}, u32[]{:S(2)}) collective-permute-start(f32[2,14,12,1]{3,2,1,0:T(8,128)} %get-tuple-element.976), channel_id=1, source_target_pairs={{0,2},{2,0},{1,3},{3,1},{4,6},{6,4},{5,7},{7,5},{8,10},{10,8},{9,1... | collective-permute-start | bytes 4040 | tf_op jit(solution)/shard_map/ppermute | solution.py:16
  184.8 2.8 collective-permute-start.17
  184.9 2.6 collective-permute-start.16
  315.8 3.9 %collective-permute-start.19 = (f32[2,14,1,130]{3,2,1,0:T(1,128)S(1)}, f32[2,14,1,130]{3,2,1,0:T(1,128)S(1)}, u32[]{:S(2)}, u32[]{:S(2)}) collective-permute-start(f32[2,14,1,130]{3,2,1,0:T(1,128)S(1)} %get-tuple-element.973), channel_id=1, source_target_pairs={{4,0},{8,4},{12,8},{0,12},{5,1},{9,5},{13,9},{1,13},{6,2},{10,6},{... | collective-permute-start | bytes 43688 | tf_op jit(solution)/shard_map/ppermute | solution.py:18
  315.8 5.7 %collective-permute-start.18 = (f32[2,14,1,130]{3,2,1,0:T(1,128)S(1)}, f32[2,14,1,130]{3,2,1,0:T(1,128)S(1)}, u32[]{:S(2)}, u32[]{:S(2)}) collective-permute-start(f32[2,14,1,130]{3,2,1,0:T(1,128)S(1)} %get-tuple-element.974), channel_id=1, source_target_pairs={{0,4},{4,8},{8,12},{12,0},{1,5},{5,9},{9,13},{13,1},{2,6},{6,10},{... | collective-permute-start | bytes 43688 | tf_op jit(solution)/shard_map/ppermute | solution.py:16
  321.8 7.2 %collective-permute-start.20 = (f32[2,14,12,1]{3,2,1,0:T(8,128)S(1)}, f32[2,14,12,1]{3,2,1,0:T(8,128)S(1)}, u32[]{:S(2)}, u32[]{:S(2)}) collective-permute-start(f32[2,14,12,1]{3,2,1,0:T(8,128)S(1)} %get-tuple-element.972), channel_id=1, source_target_pairs={{0,2},{2,0},{1,3},{3,1},{4,6},{6,4},{5,7},{7,5},{8,10},{10,8},{9,1... | collective-permute-start | bytes 4040 | tf_op jit(solution)/shard_map/ppermute | solution.py:16
  322.3 9.2 %collective-permute-start.21 = (f32[2,14,12,1]{3,2,1,0:T(8,128)S(1)}, f32[2,14,12,1]{3,2,1,0:T(8,128)S(1)}, u32[]{:S(2)}, u32[]{:S(2)}) collective-permute-start(f32[2,14,12,1]{3,2,1,0:T(8,128)S(1)} %get-tuple-element.971), channel_id=1, source_target_pairs={{2,0},{0,2},{3,1},{1,3},{6,4},{4,6},{7,5},{5,7},{10,8},{8,10},{11,... | collective-permute-start | bytes 4040 | tf_op jit(solution)/shard_map/ppermute | solution.py:18
  331.6 2.5 collective-permute-start.22
  333.6 1.4 collective-permute-start.23
  (9 other events, 25.1 us)
where the time goes:
time: 336 us
  matrix products  181 us (54%)
  blocking collectives  58.4 us (17%)
  waiting for transfers between devices  50.8 us (15%)
  starting transfers between devices  25.6 us (8%)
  other arithmetic  9.06 us (3%)
  local copies, waits for them, and re-layouts  8.45 us (3%)
    dot_general x96, matrix products, one_level(): out = jnp.dot(w_out.T, hidden, precision=HIGH) + b_out[:, None]  93.5 us
    dot_general x96, matrix products, one_level(): hidden = jnp.tanh(jnp.dot(w_in.T, block, precision=HIGH) + b_in[:, None])  87.6 us
    psum x1, blocking collectives, total_grads(): lax.psum((terms[0], terms[1], terms[2], terms[3]), ('lon', 'lat', 'lev'))  58.4 us
    ppermute x12, waiting for transfers between devices, padded_2(): lax.ppermute(tail, axis, [(i, (i + 1) % count) for i in range(count)])  37.6 us
    ppermute x12, starting transfers between devices, padded_2(): lax.ppermute(head, axis, [((i + 1) % count, i) for i in range(count)])  14.5 us
    ppermute x12, waiting for transfers between devices, padded_2(): lax.ppermute(head, axis, [((i + 1) % count, i) for i in range(count)])  13.2 us
    ppermute x12, starting transfers between devices, padded_2(): lax.ppermute(tail, axis, [(i, (i + 1) % count) for i in range(count)])  11.2 us
  transfers between devices with their start and end apart: 24, of which 19 were waited for; matrix products, arithmetic and copies ran while one was open for 2% of the time, Pallas kernels for 0%

commit v1 on v0

v1 whole, which is shorter than its diff:
```python
import jax
import jax.numpy as jnp
from jax import lax
from jax.experimental import pallas as pl
from jax.experimental.pallas import tpu as pltpu
from jax.sharding import PartitionSpec as P

MESH = pl.DeviceIdType.MESH
BF = jnp.bfloat16
F32 = jnp.float32
AXES = ("lev", "lon", "lat")
DIRECT = 16


def halves(x):
    hi = x.astype(BF).astype(F32)
    return hi, x - hi


def split(x):
    hi = x.astype(BF)
    return hi, (x - hi.astype(F32)).astype(BF)


def make_kernel(sizes, nz, hid, factor):
    total = sizes["lev"] * sizes["lon"] * sizes["lat"]
    groups = (AXES,) if total <= DIRECT else tuple((a,) for a in AXES)

    def group_size(group):
        n = 1
        for a in group:
            n *= sizes[a]
        return n

    def my_rank(group):
        me = 0
        for a in group:
            me = me * sizes[a] + lax.axis_index(a)
        return me

    def device_of(group, rank):
        where = {}
        for a in reversed(group):
            where[a] = lax.rem(rank, sizes[a])
            rank = rank // sizes[a]
        return where

    def kernel(state, land, east, north, cot, prm, gs, gp, *scratch):
        halo = [scratch[6 * p : 6 * p + 6] for p in range(4)]
        feats = scratch[24:26]
        nets = scratch[26:28]
        douts = scratch[28:30]
        near, rates, acc, small, slots = scratch[30:35]
        send_sem, recv_sem, sum_send, sum_recv = scratch[35:39]

        barrier = pltpu.get_barrier_semaphore()
        peers = 0
        for group in groups:
            n = group_size(group)
            me = my_rank(group)
            for d in range(1, n):
                pl.semaphore_signal(
                    barrier, inc=1, device_id=device_of(group, lax.rem(me + d, n)), device_id_type=MESH
                )
                peers += 1
        pl.semaphore_wait(barrier, peers)

        sub = lax.broadcasted_iota(jnp.int32, (1, 8, 128), 1)
        lane = lax.broadcasted_iota(jnp.int32, (1, 8, 128), 2)
        lane2 = lax.broadcasted_iota(jnp.int32, (8, 128), 1)

        def flag(cond):
            return jnp.where(cond, 1.0, 0.0).astype(F32)

        lev, lat = lax.axis_index("lev"), lax.axis_index("lat")
        ends = {
            "lev": (flag(lev > 0), flag(lev < sizes["lev"] - 1)),
            "lat": (flag(lat > 0), flag(lat < sizes["lat"] - 1)),
            "lon": (None, None),
        }

        def begin(p, zlo, zhi, xlo, xhi, ylo, yhi):
            sz, sx, sy, rz, rx, ry = halo[p]
            count = zlo.shape[0]
            sz[0] = zlo[:, 0]
            sz[1] = zhi[:, nz - 1]
            sx[0] = xlo[:, :, 0:1, :].reshape(count * nz, 1, 128)
            sx[1] = xhi[:, :, 7:8, :].reshape(count * nz, 1, 128)
            for side, field, at in ((0, ylo, 0), (1, yhi, 127)):
                packed = jnp.zeros((8, 128), F32)
                for t in range(count):
                    for z in range(nz):
                        packed = jnp.where(lane2 == t * nz + z, field[t, z][:, at : at + 1], packed)
                sy[side] = packed
            copies = []
            for k, (axis, src, dst) in enumerate((("lev", sz, rz), ("lon", sx, rx), ("lat", sy, ry))):
                n = sizes[axis]
                i = lax.axis_index(axis)
                for side in (0, 1):
                    to = lax.rem(i + (n - 1 if side == 0 else 1), n)
                    copy = pltpu.make_async_remote_copy(
                        src_ref=src.at[side],
                        dst_ref=dst.at[1 - side],
                        send_sem=send_sem.at[p, 2 * k + side],
                        recv_sem=recv_sem.at[p, 2 * k + 1 - side],
                        device_id={axis: to},
                        device_id_type=MESH,
                    )
                    copy.start()
                    copies.append(copy)
            return copies

        def finish(copies):
            for copy in copies:
                copy.wait()

        def closed(x, axis, side, close):
            return x * ends[axis][side] if close else x

        def up(p, c, close):
            rz = halo[p][3]
            return jnp.concatenate([c[:, 1:], closed(rz[1], "lev", 1, close)[:, None]], 1)

        def down(p, c, close):
            rz = halo[p][3]
            return jnp.concatenate([closed(rz[0], "lev", 0, close)[:, None], c[:, :-1]], 1)

        def lon_shift(p, c, side):
            rx = halo[p][4]
            flat = c.reshape(-1, 8, 128)
            rolled = pltpu.roll(flat, 7 if side == 1 else 1, 1)
            return jnp.where(sub == (7 if side == 1 else 0), rx[side], rolled).reshape(c.shape)

        def lat_shift(p, c, side, close):
            ry = halo[p][5]
            packed = closed(ry[side], "lat", side, close)
            flat = c.reshape(-1, 8, 128)
            edge = jnp.stack(
                [jnp.broadcast_to(packed[:, i : i + 1], (8, 128)) for i in range(flat.shape[0])]
            )
            rolled = pltpu.roll(flat, 127 if side == 1 else 1, 2)
            return jnp.where(lane == (127 if side == 1 else 0), edge, rolled).reshape(c.shape)

        def around(p, c, close):
            return (
                up(p, c, close),
                down(p, c, close),
                lon_shift(p, c, 1),
                lon_shift(p, c, 0),
                lat_shift(p, c, 1, close),
                lat_shift(p, c, 0, close),
            )

        mask = land[...].astype(F32)
        first = jnp.concatenate([state[...], mask[None]], 0)
        copies = begin(0, *((first,) * 6))

        rows = prm[...]
        w_hi, w_lo = halves(rows[0:8])
        lhs = jnp.concatenate([w_hi, w_hi, w_lo, w_lo, jnp.zeros((96, hid), F32)], 0)
        w_rows = lhs.T[:, :32].astype(BF)
        wo0, wo1 = rows[8:9], rows[9:10]
        row16 = lax.broadcasted_iota(jnp.int32, (16, hid), 0)
        six = lax.broadcasted_iota(jnp.int32, (8, hid), 0) < 6
        prods = jnp.concatenate(
            [jnp.where(six, rows[0:8] * wo0, 0.0), jnp.where(six, rows[0:8] * wo1, 0.0)], 0
        )
        outs = jnp.where(row16 == 6, wo0, 0.0) + jnp.where(row16 == 7, wo1, 0.0)
        g_lhs = jnp.concatenate(halves(prods), 0).astype(BF)
        h_lhs = jnp.concatenate(halves(outs), 0).astype(BF)
        bias0 = rows[10:11, 0:128].reshape(1, 1, 128)
        bias1 = rows[11:12, 0:128].reshape(1, 1, 128)

        finish(copies)
        m_near = around(0, first, True)
        for k in range(6):
            near[k] = m_near[k][2]

        def stencil(c, neighbours):
            flux = [near[k][None] * (neighbours[k] - c) for k in range(6)]
            return flux

        def features(step, c, neighbours):
            flux = stencil(c, neighbours)
            vertical = flux[0] + flux[1]
            horizontal = flux[2] + flux[3] + flux[4] + flux[5]
            ft = feats[step]
            for k, pair in enumerate((c, vertical, horizontal)):
                for t in range(2):
                    ft[:, 2 * k + t] = pair[t]
            ft[:, 6] = jnp.ones((nz, 8, 128), F32)
            ft[:, 7] = jnp.zeros((nz, 8, 128), F32)
            return flux

        def cell_rows(step, z):
            return jnp.swapaxes(feats[step][z], 0, 1)

        def hidden(cells):
            hi, lo = halves(cells)
            stacked = jnp.concatenate([hi, lo, hi, lo], 1).astype(BF)
            for pair in range(4):
                rhs = jnp.concatenate([stacked[2 * pair], stacked[2 * pair + 1]], 1)
                h = jnp.tanh(jnp.dot(w_rows, rhs, preferred_element_type=F32))
                g = 1.0 - h * h
                yield pair, split(h), split(g)

        def network(step):
            def level(z, carry):
                out = []
                for pair, h, g in hidden(cell_rows(step, z)):
                    res = (
                        jnp.dot(h_lhs, h[0], preferred_element_type=F32)
                        + jnp.dot(h_lhs, h[1], preferred_element_type=F32)
                        + jnp.dot(g_lhs, g[0], preferred_element_type=F32)
                        + jnp.dot(g_lhs, g[1], preferred_element_type=F32)
                    )
                    res = res[0:16] + res[16:32]
                    out += [res[:, 0:128], res[:, 128:256]]
                lower = jnp.stack([o[0:8] for o in out])
                upper = jnp.stack([o[8:16] for o in out])
                nets[step][z, 0:8] = jnp.swapaxes(lower, 0, 1)
                nets[step][z, 8:16] = jnp.swapaxes(upper, 0, 1)
                return carry

            lax.fori_loop(0, nz, level, 0)

        def sigmoids(step):
            net = nets[step]
            s0 = jax.nn.sigmoid(net[:, 6] + bias0)
            s1 = jax.nn.sigmoid(net[:, 7] + bias1)
            return s0, s1

        def winds():
            u, v = east[...], north[...]
            return (
                -jnp.minimum(u, 0.0),
                jnp.maximum(u, 0.0),
                -jnp.minimum(v, 0.0),
                jnp.maximum(v, 0.0),
            )

        c0 = state[...]
        flux = features(0, c0, [m[0:2] for m in m_near])
        wind = winds()
        advect = sum(wind[k][None] * flux[2 + k] for k in range(4))
        rates[...] = advect
        network(0)
        s0, s1 = sigmoids(0)
        ft = feats[0]
        move = jnp.stack(
            [0.08 * s0 * ft[:, 4 + t] + 0.16 * s1 * ft[:, 2 + t] + rates[t] for t in range(2)]
        )
        c1 = c0 + mask[None] * move
        copies = begin(1, *((c1,) * 6))
        finish(copies)
        features(1, c1, around(1, c1, False))
        network(1)

        def local_adjoint(step, lam):
            s0, s1 = sigmoids(step)
            ft, net = feats[step], nets[step]
            r = [mask * lam[t] for t in range(2)]
            d0 = (r[0] * ft[:, 4] + r[1] * ft[:, 5]) * (0.08 * s0 * (1.0 - s0))
            d1 = (r[0] * ft[:, 2] + r[1] * ft[:, 3]) * (0.16 * s1 * (1.0 - s1))
            douts[step][0] = d0
            douts[step][1] = d1
            back = [d0 * net[:, f] + d1 * net[:, 8 + f] for f in range(6)]
            center = jnp.stack([lam[t] + back[t] for t in range(2)])
            vert = jnp.stack([r[t] * (0.16 * s1) + back[2 + t] for t in range(2)])
            hor = [r[t] * (0.08 * s0) + back[4 + t] for t in range(2)]
            wind = winds()
            sides = [jnp.stack([hor[t] + wind[k] * r[t] for t in range(2)]) for k in range(4)]
            own = center - vert * (near[0] + near[1])[None]
            for k in range(4):
                own = own - sides[k] * near[2 + k][None]
            return own, vert, sides

        def gathered(p, own, vert, sides):
            e, w, n, s = sides
            came = (
                up(p, vert, True)
                + down(p, vert, True)
                + lon_shift(p, w, 1)
                + lon_shift(p, e, 0)
                + lat_shift(p, s, 1, True)
                + lat_shift(p, n, 0, True)
            )
            return own + mask[None] * came

        def weight_terms(step):
            row8 = lax.broadcasted_iota(jnp.int32, (8, 128), 0)

            def level(z, carry):
                cells = cell_rows(step, z)
                d0, d1 = douts[step][0, z], douts[step][1, z]
                g_rows, h_rows = [], []
                for s in range(8):
                    a = jnp.broadcast_to(d0[s : s + 1], (8, 128))
                    b = jnp.broadcast_to(d1[s : s + 1], (8, 128))
                    pair = jnp.concatenate([a * cells[s], b * cells[s]], 0)
                    g_rows.append(jnp.concatenate(halves(pair), 0))
                    pair = jnp.concatenate(
                        [jnp.where(row8 == 7, a, 0.0), jnp.where(row8 == 7, b, 0.0)], 0
                    )
                    h_rows.append(jnp.concatenate(halves(pair), 0))
                total_rows = jnp.zeros((32, hid), F32)
                for pair, h, g in hidden(cells):
                    gl = jnp.concatenate(g_rows[2 * pair : 2 * pair + 2], 1).astype(BF)
                    hl = jnp.concatenate(h_rows[2 * pair : 2 * pair + 2], 1).astype(BF)
                    for left, right in ((hl, h[0]), (hl, h[1]), (gl, g[0]), (gl, g[1])):
                        total_rows += lax.dot_general(
                            left, right, (((1,), (1,)), ((), ())), preferred_element_type=F32
                        )
                acc[...] += total_rows[0:16] + total_rows[16:32]
                return carry

            lax.fori_loop(0, nz, level, 0)

        own, vert, sides = local_adjoint(1, cot[...])
        copies = begin(2, vert, vert, sides[1], sides[0], sides[3], sides[2])
        acc[...] = jnp.zeros((16, hid), F32)
        weight_terms(1)
        finish(copies)
        lam = gathered(2, own, vert, sides)

        own, vert, sides = local_adjoint(0, lam)
        copies = begin(3, vert, vert, sides[1], sides[0], sides[3], sides[2])
        weight_terms(0)
        terms = acc[...]
        both = [jnp.sum(douts[0][o] + douts[1][o], axis=0) for o in range(2)]
        both = [jnp.sum(jnp.sum(b, axis=0, keepdims=True), axis=1, keepdims=True) for b in both]
        lane_h = lax.broadcasted_iota(jnp.int32, (1, hid), 1)
        last = jnp.where(lane_h == 0, both[0], 0.0) + jnp.where(lane_h == 1, both[1], 0.0)
        joined = jnp.concatenate(
            [
                terms[0:7] * wo0 + terms[8:15] * wo1,
                terms[7:8],
                terms[15:16],
                last,
                jnp.zeros((6, hid), F32),
            ],
            0,
        )
        small[0] = joined * factor

        used = 0
        for index, group in enumerate(groups):
            n = group_size(group)
            me = my_rank(group)
            slots[used + me] = small[index]
            out_copies = []
            for d in range(1, n):
                copy = pltpu.make_async_remote_copy(
                    src_ref=small.at[index],
                    dst_ref=slots.at[used + me],
                    send_sem=sum_send.at[used + d],
                    recv_sem=sum_recv.at[used + me],
                    device_id=device_of(group, lax.rem(me + d, n)),
                    device_id_type=MESH,
                )
                copy.start()
                out_copies.append(copy)
            if index == 0:
                finish(copies)
                gs[...] = gathered(3, own, vert, sides)
            for d in range(1, n):
                source = lax.rem(me + d, n)
                pltpu.make_async_remote_copy(
                    src_ref=small.at[index],
                    dst_ref=slots.at[used + source],
                    send_sem=sum_send.at[used + d],
                    recv_sem=sum_recv.at[used + source],
                    device_id=device_of(group, source),
                    device_id_type=MESH,
                ).wait_recv()
            for copy in out_copies:
                copy.wait_send()
            value = slots[used]
            for k in range(1, n):
                value = value + slots[used + k]
            used += n
            if index == len(groups) - 1:
                gp[...] = value
            else:
                small[index + 1] = value

    total_slots = sum(group_size(g) for g in groups)
    cell = lambda *lead: pltpu.VMEM((*lead, 8, 128), F32)
    scratch = []
    for count in (3, 2, 2, 2):
        scratch += [cell(2, count), pltpu.VMEM((2, count * nz, 1, 128), F32), cell(2)] * 2
    scratch += [cell(nz, 8)] * 2 + [cell(nz, 16)] * 2 + [cell(2, nz)] * 2
    scratch += [
        cell(6, nz),
        cell(2, nz),
        pltpu.VMEM((16, hid), F32),
        pltpu.VMEM((len(groups), 16, hid), F32),
        pltpu.VMEM((total_slots, 16, hid), F32),
        pltpu.SemaphoreType.DMA((4, 6)),
        pltpu.SemaphoreType.DMA((4, 6)),
        pltpu.SemaphoreType.DMA((total_slots,)),
        pltpu.SemaphoreType.DMA((total_slots,)),
    ]
    return kernel, scratch


def solution(mesh):
    sizes = {a: mesh.shape[a] for a in AXES}

    def per_device(state, land_sea, east_speed, north_speed, w_in, b_in, w_out, b_out, cotangent):
        nz = state.shape[1]
        hid = w_in.shape[1]
        cells = state.shape[1] * state.shape[2] * state.shape[3]
        cells *= sizes["lev"] * sizes["lon"] * sizes["lat"]
        kernel, scratch = make_kernel(sizes, nz, hid, float(cells) ** (-0.5))
        prm = jnp.concatenate(
            [
                w_in,
                b_in[None],
                jnp.zeros((1, hid), F32),
                w_out.T,
                jnp.broadcast_to(b_out[:, None], (2, hid)),
                jnp.zeros((4, hid), F32),
            ],
            0,
        )
        vmem = pl.BlockSpec(memory_space=pltpu.VMEM)
        grad, par = pl.pallas_call(
            kernel,
            out_shape=(
                jax.ShapeDtypeStruct(state.shape, F32),
                jax.ShapeDtypeStruct((16, hid), F32),
            ),
            in_specs=[vmem] * 6,
            out_specs=(vmem, vmem),
            scratch_shapes=scratch,
            compiler_params=pltpu.CompilerParams(
                collective_id=0, has_side_effects=True, vmem_limit_bytes=48 * 1024 * 1024
            ),
        )(state, land_sea, east_speed, north_speed, cotangent, prm)
        return grad, par[0:6], par[6], par[7:9].T, par[9, 0:2]

    placed = (
        P("ens", "lev", "lon", "lat"),
        P("lev", "lon", "lat"),
        P(("ens", "lev"), "lon", "lat"),
        P(("ens", "lev"), "lon", "lat"),
        P(),
        P(),
        P(),
        P(),
        P("ens", "lev", "lon", "lat"),
    )
    return jax.shard_map(
        per_device,
        mesh=mesh,
        in_specs=placed,
        out_specs=(
            P("ens", "lev", "lon", "lat"),
            P("ens", None),
            P("ens"),
            P("ens", None),
            P("ens"),
        ),
        check_vma=False,
    )
```

time: 336 us -> 78.3 us (0.23)
  matrix products: 181 us -> 0 us
  Pallas kernels: 0 us -> 68.7 us
  blocking collectives: 58.4 us -> 0 us
  waiting for transfers between devices: 50.8 us -> 0 us
  starting transfers between devices: 25.6 us -> 0 us
  other arithmetic: 9.06 us -> 0 us
    dot_general x192 -> x0, matrix products: 181 us -> none  [the longest x96 93.5 us: one_level(): out = jnp.dot(w_out.T, hidden, precision=HIGH) + b_out[:, None]]
    pallas_call x0 -> x1, Pallas kernels: none -> 68.7 us  [per_device(): pl.pallas_call(kernel, out_shape=(jax.ShapeDtypeStruct(state.shape, F32),...]
    psum x1 -> x0, blocking collectives: 58.4 us -> none  [total_grads(): lax.psum((terms[0], terms[1], terms[2], terms[3]), ('lon', 'lat', 'lev'))]
    ppermute x24 -> x0, waiting for transfers between devices: 50.8 us -> none  [the longest x12 37.6 us: padded_2(): lax.ppermute(tail, axis, [(i, (i + 1) % count) for i in range(count)])]
    ppermute x24 -> x0, starting transfers between devices: 25.6 us -> none  [the longest x12 14.5 us: padded_2(): lax.ppermute(head, axis, [((i + 1) % count, i) for i in range(count)])]
    scatter-add x8 -> x0, local copies, waits for them, and re-layouts: 4.48 us -> none  [the longest x2 3.81 us: fold_back(): inner = inner.at[:, :, :, -1].add(ext[:, 2:-2, 2:-2, -1])]
    unnamed x18 -> x17, local copies, waits for them, and re-layouts: 1.37 us -> 5.5 us
  transfers between devices with their start and end apart: 24 -> 0, of which waited for: 19 -> 0; matrix products, arithmetic and copies ran while one was open for 2% -> 0% of each run, Pallas kernels for 0% -> 0%
where the time goes in v1:
time: 78.3 us; the launch traced here: 77.9 us
  Pallas kernels  68.7 us (88%)
  local copies, waits for them, and re-layouts  8.53 us (11%)
    pallas_call x1, Pallas kernels, per_device(): pl.pallas_call(kernel, out_shape=(jax.ShapeDtypeStruct(state.shape, F32),...  68.7 us
    unnamed x17, local copies, waits for them, and re-layouts  5.5 us

profile of v1, /device:TPU:0, one launch (start us, length us, event | category | flops | bytes accessed | tf_op | source)
XLA Modules:
  0.0 77.9 jit_solution(12165889139189102280)
XLA Ops:
  0.6 0.0 copy-start.5
  0.6 0.7 broadcast_in_dim.17
  1.4 0.0 copy-start.6
  1.4 0.0 copy-start.7
  1.4 0.0 copy-done.5
  1.4 0.7 copy-done.6
  2.1 0.0 copy-done.7
  2.1 0.0 copy-start
  2.1 0.9 %copy-done = f32[2,12,8,128]{3,2,1,0:T(8,128)S(1)} copy-done((f32[2,12,8,128]{3,2,1,0:T(8,128)S(1)}, f32[2,12,8,128]{3,2,1,0:T(8,128)}, u32[]{:S(2)}) %copy-start) | copy-done | bytes 98328
  3.0 0.0 copy-start.1
  3.0 0.9 %copy-done.1 = f32[2,12,8,128]{3,2,1,0:T(8,128)S(1)} copy-done((f32[2,12,8,128]{3,2,1,0:T(8,128)S(1)}, f32[2,12,8,128]{3,2,1,0:T(8,128)}, u32[]{:S(2)}) %copy-start.1) | copy-done | bytes 98328
  3.9 0.0 copy-start.2
  3.9 0.8 %copy-done.2 = s32[12,8,128]{2,1,0:T(8,128)S(1)} copy-done((s32[12,8,128]{2,1,0:T(8,128)S(1)}, s32[12,8,128]{2,1,0:T(8,128)}, u32[]{:S(2)}) %copy-start.2) | copy-done | bytes 49176
  4.7 0.0 copy-start.3
  4.7 0.8 %copy-done.3 = f32[12,8,128]{2,1,0:T(8,128)S(1)} copy-done((f32[12,8,128]{2,1,0:T(8,128)S(1)}, f32[12,8,128]{2,1,0:T(8,128)}, u32[]{:S(2)}) %copy-start.3) | copy-done | bytes 49176
  5.5 0.0 copy-start.4
  5.5 0.8 %copy-done.4 = f32[12,8,128]{2,1,0:T(8,128)S(1)} copy-done((f32[12,8,128]{2,1,0:T(8,128)S(1)}, f32[12,8,128]{2,1,0:T(8,128)}, u32[]{:S(2)}) %copy-start.4) | copy-done | bytes 49176
  6.3 68.7 %shard_map.128 = (f32[2,12,8,128]{3,2,1,0:T(8,128)S(1)}, f32[16,256]{1,0:T(8,128)S(1)}) custom-call(f32[2,12,8,128]{3,2,1,0:T(8,128)S(1)} %copy-done, s32[12,8,128]{2,1,0:T(8,128)S(1)} %copy-done.2, f32[12,8,128]{2,1,0:T(8,128)S(1)} %copy-done.3, f32[12,8,128]{2,1,0:T(8,128)S(1)} %copy-done.4, f32[2,12,8,128]{3,2,1,0:T(8,128)S(1)} %copy-done.1, ...), custom_call_target="tpu_custom_call" | custom-call | tf_op jit(solution)/shard_map/pallas_call | solution.py:428
  75.0 0.6 slice.12
  75.6 0.6 slice_bitcast_fusion
  76.2 0.6 slice.13
  76.8 0.5 slice_bitcast_fusion.1
  77.3 0.6 copy.15
  (3 shorter events, 0.0 us)
Async XLA Ops:
  0.6 0.8 copy-start.5
  1.4 0.7 copy-start.6
  1.4 0.7 copy-start.7
  2.1 0.9 %copy-start = (f32[2,12,8,128]{3,2,1,0:T(8,128)S(1)}, f32[2,12,8,128]{3,2,1,0:T(8,128)}, u32[]{:S(2)}) copy-start(f32[2,12,8,128]{3,2,1,0:T(8,128)} %state.1) | copy-start | bytes 294916
  3.0 0.9 %copy-start.1 = (f32[2,12,8,128]{3,2,1,0:T(8,128)S(1)}, f32[2,12,8,128]{3,2,1,0:T(8,128)}, u32[]{:S(2)}) copy-start(f32[2,12,8,128]{3,2,1,0:T(8,128)} %cot.1) | copy-start | bytes 294916
  3.9 0.8 %copy-start.2 = (s32[12,8,128]{2,1,0:T(8,128)S(1)}, s32[12,8,128]{2,1,0:T(8,128)}, u32[]{:S(2)}) copy-start(s32[12,8,128]{2,1,0:T(8,128)} %land.1) | copy-start | bytes 147460
  4.7 0.8 %copy-start.3 = (f32[12,8,128]{2,1,0:T(8,128)S(1)}, f32[12,8,128]{2,1,0:T(8,128)}, u32[]{:S(2)}) copy-start(f32[12,8,128]{2,1,0:T(8,128)} %east.1) | copy-start | bytes 147460
  5.5 0.8 %copy-start.4 = (f32[12,8,128]{2,1,0:T(8,128)S(1)}, f32[12,8,128]{2,1,0:T(8,128)}, u32[]{:S(2)}) copy-start(f32[12,8,128]{2,1,0:T(8,128)} %north.1) | copy-start | bytes 147460

commit v2 on v1

--- a/solution.py
+++ b/solution.py
@@ -45,7 +45,15 @@
             rank = rank // sizes[a]
         return where
 
-    def kernel(state, land, east, north, cot, prm, gs, gp, *scratch):
+    def kernel(*refs):
+        sources, (gs, g_in, g_bin, g_out, g_bout), scratch = refs[0:9], refs[9:14], refs[14:]
+        state, land, east, north, cot, w_in, b_in, w_out, b_out = scratch[39:48]
+        load_sem = scratch[48]
+        loads = [
+            pltpu.make_async_copy(sources[k], scratch[39 + k], load_sem.at[k]) for k in range(9)
+        ]
+        for load in loads:
+            load.start()
         halo = [scratch[6 * p : 6 * p + 6] for p in range(4)]
         feats = scratch[24:26]
         nets = scratch[26:28]
@@ -151,26 +159,33 @@
                 lat_shift(p, c, 0, close),
             )
 
+        loads[0].wait()
+        loads[1].wait()
         mask = land[...].astype(F32)
         first = jnp.concatenate([state[...], mask[None]], 0)
         copies = begin(0, *((first,) * 6))
 
-        rows = prm[...]
-        w_hi, w_lo = halves(rows[0:8])
+        for k in range(5, 9):
+            loads[k].wait()
+        rows = jnp.concatenate([w_in[...], b_in[...], jnp.zeros((1, hid), F32)], 0)
+        w_hi, w_lo = halves(rows)
         lhs = jnp.concatenate([w_hi, w_hi, w_lo, w_lo, jnp.zeros((96, hid), F32)], 0)
         w_rows = lhs.T[:, :32].astype(BF)
-        wo0, wo1 = rows[8:9], rows[9:10]
+        wo0, wo1 = w_out[0:1], w_out[1:2]
         row16 = lax.broadcasted_iota(jnp.int32, (16, hid), 0)
         six = lax.broadcasted_iota(jnp.int32, (8, hid), 0) < 6
         prods = jnp.concatenate(
-            [jnp.where(six, rows[0:8] * wo0, 0.0), jnp.where(six, rows[0:8] * wo1, 0.0)], 0
+            [jnp.where(six, rows * wo0, 0.0), jnp.where(six, rows * wo1, 0.0)], 0
         )
         outs = jnp.where(row16 == 6, wo0, 0.0) + jnp.where(row16 == 7, wo1, 0.0)
         g_lhs = jnp.concatenate(halves(prods), 0).astype(BF)
         h_lhs = jnp.concatenate(halves(outs), 0).astype(BF)
-        bias0 = rows[10:11, 0:128].reshape(1, 1, 128)
-        bias1 = rows[11:12, 0:128].reshape(1, 1, 128)
-
+        bias0 = jnp.broadcast_to(b_out[:, 0:1], (8, 128))[None]
+        bias1 = jnp.broadcast_to(b_out[:, 1:2], (8, 128))[None]
+
+        loads[2].wait()
+        loads[3].wait()
+        loads[4].wait()
         finish(copies)
         m_near = around(0, first, True)
         for k in range(6):
@@ -303,22 +318,25 @@
                         [jnp.where(row8 == 7, a, 0.0), jnp.where(row8 == 7, b, 0.0)], 0
                     )
                     h_rows.append(jnp.concatenate(halves(pair), 0))
-                total_rows = jnp.zeros((32, hid), F32)
+                lefts, rights = [], []
                 for pair, h, g in hidden(cells):
                     gl = jnp.concatenate(g_rows[2 * pair : 2 * pair + 2], 1).astype(BF)
                     hl = jnp.concatenate(h_rows[2 * pair : 2 * pair + 2], 1).astype(BF)
-                    for left, right in ((hl, h[0]), (hl, h[1]), (gl, g[0]), (gl, g[1])):
-                        total_rows += lax.dot_general(
-                            left, right, (((1,), (1,)), ((), ())), preferred_element_type=F32
-                        )
-                acc[...] += total_rows[0:16] + total_rows[16:32]
+                    lefts += [h[0], h[1], g[0], g[1]]
+                    rights += [hl, hl, gl, gl]
+                acc[...] += lax.dot_general(
+                    jnp.concatenate(lefts, 1),
+                    jnp.concatenate(rights, 1),
+                    (((1,), (1,)), ((), ())),
+                    preferred_element_type=F32,
+                )
                 return carry
 
             lax.fori_loop(0, nz, level, 0)
 
         own, vert, sides = local_adjoint(1, cot[...])
         copies = begin(2, vert, vert, sides[1], sides[0], sides[3], sides[2])
-        acc[...] = jnp.zeros((16, hid), F32)
+        acc[...] = jnp.zeros((hid, 32), F32)
         weight_terms(1)
         finish(copies)
         lam = gathered(2, own, vert, sides)
@@ -326,7 +344,8 @@
         own, vert, sides = local_adjoint(0, lam)
         copies = begin(3, vert, vert, sides[1], sides[0], sides[3], sides[2])
         weight_terms(0)
-        terms = acc[...]
+        terms = jnp.concatenate([acc[...], jnp.zeros((hid, 96), F32)], 1).T
+        terms = terms[0:16] + terms[16:32]
         both = [jnp.sum(douts[0][o] + douts[1][o], axis=0) for o in range(2)]
         both = [jnp.sum(jnp.sum(b, axis=0, keepdims=True), axis=1, keepdims=True) for b in both]
         lane_h = lax.broadcasted_iota(jnp.int32, (1, hid), 1)
@@ -380,7 +399,10 @@
                 value = value + slots[used + k]
             used += n
             if index == len(groups) - 1:
-                gp[...] = value
+                g_in[...] = value[0:6]
+                g_bin[...] = value[6:7]
+                g_out[...] = value[7:9]
+                g_bout[...] = value[9:10, 0:2]
             else:
                 small[index + 1] = value
 
@@ -393,15 +415,34 @@
     scratch += [
         cell(6, nz),
         cell(2, nz),
-        pltpu.VMEM((16, hid), F32),
+        pltpu.VMEM((hid, 32), F32),
         pltpu.VMEM((len(groups), 16, hid), F32),
         pltpu.VMEM((total_slots, 16, hid), F32),
         pltpu.SemaphoreType.DMA((4, 6)),
         pltpu.SemaphoreType.DMA((4, 6)),
         pltpu.SemaphoreType.DMA((total_slots,)),
         pltpu.SemaphoreType.DMA((total_slots,)),
+        cell(2, nz),
+        pltpu.VMEM((nz, 8, 128), jnp.int32),
+        cell(nz),
+        cell(nz),
+        cell(2, nz),
+        pltpu.VMEM((6, hid), F32),
+        pltpu.VMEM((1, hid), F32),
+        pltpu.VMEM((2, hid), F32),
+        pltpu.VMEM((1, 2), F32),
+        pltpu.SemaphoreType.DMA((9,)),
     ]
     return kernel, scratch
+
+
+def hand_over(*refs):
+    sem = refs[10]
+    copies = [pltpu.make_async_copy(refs[k], refs[5 + k], sem.at[k]) for k in range(5)]
+    for copy in copies:
+        copy.start()
+    for copy in copies:
+        copy.wait()
 
 
 def solution(mesh):
@@ -413,32 +454,44 @@
         cells = state.shape[1] * state.shape[2] * state.shape[3]
         cells *= sizes["lev"] * sizes["lon"] * sizes["lat"]
         kernel, scratch = make_kernel(sizes, nz, hid, float(cells) ** (-0.5))
-        prm = jnp.concatenate(
-            [
-                w_in,
-                b_in[None],
-                jnp.zeros((1, hid), F32),
-                w_out.T,
-                jnp.broadcast_to(b_out[:, None], (2, hid)),
-                jnp.zeros((4, hid), F32),
-            ],
-            0,
+        vmem = pl.BlockSpec(memory_space=pltpu.VMEM)
+        shapes = (
+            jax.ShapeDtypeStruct(state.shape, F32),
+            jax.ShapeDtypeStruct((6, hid), F32),
+            jax.ShapeDtypeStruct((1, hid), F32),
+            jax.ShapeDtypeStruct((2, hid), F32),
+            jax.ShapeDtypeStruct((1, 2), F32),
         )
-        vmem = pl.BlockSpec(memory_space=pltpu.VMEM)
-        grad, par = pl.pallas_call(
+        results = pl.pallas_call(
             kernel,
-            out_shape=(
-                jax.ShapeDtypeStruct(state.shape, F32),
-                jax.ShapeDtypeStruct((16, hid), F32),
-            ),
-            in_specs=[vmem] * 6,
-            out_specs=(vmem, vmem),
+            out_shape=shapes,
+            in_specs=[pl.BlockSpec(memory_space=pl.ANY)] * 9,
+            out_specs=(vmem,) * 5,
             scratch_shapes=scratch,
             compiler_params=pltpu.CompilerParams(
-                collective_id=0, has_side_effects=True, vmem_limit_bytes=48 * 1024 * 1024
+                collective_id=0, has_side_effects=True, vmem_limit_bytes=60 * 1024 * 1024
             ),
-        )(state, land_sea, east_speed, north_speed, cotangent, prm)
-        return grad, par[0:6], par[6], par[7:9].T, par[9, 0:2]
+        )(
+            state,
+            land_sea,
+            east_speed,
+            north_speed,
+            cotangent,
+            w_in,
+            b_in[None],
+            w_out.T,
+            b_out[None],
+        )
+        anywhere = pl.BlockSpec(memory_space=pl.ANY)
+        grad, g_in, g_bin, g_out, g_bout = pl.pallas_call(
+            hand_over,
+            out_shape=shapes,
+            in_specs=[anywhere] * 5,
+            out_specs=(anywhere,) * 5,
+            scratch_shapes=[pltpu.SemaphoreType.DMA((5,))],
+            compiler_params=pltpu.CompilerParams(vmem_limit_bytes=60 * 1024 * 1024),
+        )(*results)
+        return grad, g_in, g_bin[0], g_out.T, g_bout[0]
 
     placed = (
         P("ens", "lev", "lon", "lat"),

time: 78.3 us -> 67.5 us (0.86)
  local copies, waits for them, and re-layouts: 8.53 us -> 0 us
  Pallas kernels: 68.7 us -> 66.8 us
    unnamed x17 -> x0, local copies, waits for them, and re-layouts: 5.5 us -> none
    pallas_call x1 -> x2, Pallas kernels: 68.7 us -> 66.8 us  [the longest x1 62.3 us: per_device(): pl.pallas_call(kernel, out_shape=shapes, in_specs=[pl.BlockSpec(memory_sp...]
    slice x2 -> x0, local copies, waits for them, and re-layouts: 1.17 us -> none  [per_device(): return (grad, par[0:6], par[6], par[7:9].T, par[9, 0:2])]
where the time goes in v2:
time: 67.5 us; the launch traced here: 67.4 us
  Pallas kernels  66.8 us (99%)
    pallas_call x1, Pallas kernels, per_device(): pl.pallas_call(kernel, out_shape=shapes, in_specs=[pl.BlockSpec(memory_sp...  62.3 us
    pallas_call x1, Pallas kernels, per_device(): pl.pallas_call(hand_over, out_shape=shapes, in_specs=[anywhere] * 5, out_...  4.48 us

profile of v2, /device:TPU:0, one launch (start us, length us, event | category | flops | bytes accessed | tf_op | source)
XLA Modules:
  0.0 67.4 jit_solution(7349455934903587499)
XLA Ops:
  0.6 62.3 %shard_map.128 = (f32[2,12,8,128]{3,2,1,0:T(8,128)}, f32[6,256]{1,0:T(8,128)}, f32[1,256]{1,0:T(1,128)}, f32[2,256]{1,0:T(2,128)}, f32[1,2]{1,0:T(1,128)}) custom-call(f32[2,12,8,128]{3,2,1,0:T(8,128)} %refs_0_.1, s32[12,8,128]{2,1,0:T(8,128)} %refs_1_.1, f32[12,8,128]{2,1,0:T(8,128)} %refs_2_.1, f32[12,8,128]{2,1,0:T(8,128)} %refs_3_.1, ...), custom_call_target="tpu_custom_call" | custom-call | tf_op jit(solution)/shard_map/pallas_call | solution.py:465
  62.9 4.5 %shard_map.129 = (f32[2,12,8,128]{3,2,1,0:T(8,128)}, f32[6,256]{1,0:T(8,128)}, f32[1,256]{1,0:T(1,128)}, f32[2,256]{1,0:T(2,128)}, f32[1,2]{1,0:T(1,128)}) custom-call(f32[2,12,8,128]{3,2,1,0:T(8,128)} %get-tuple-element.15.refs_0_, f32[6,256]{1,0:T(8,128)} %get-tuple-element.16.refs_1_, f32[1,256]{1,0:T(1,128)} %get-tuple-element.17.refs_2_, ...), custom_call_target="tpu_custom_call" | custom-call | tf_op jit(solution)/shard_map/pallas_call | solution.py:486
